TPU v7x, 256 devices: a whole 4x4x8 slice. The times are simulated.
256 devices in a mesh: gx: 32 (over y, z_lo, x), gz: 8 (over z_hi, core).
Axes of the slice: x: 4, y: 4, z: 8 (z_hi: 4, z_lo: 2; z = z_hi * 2 + z_lo), core: 2. Of those that a mesh axis runs over, the one named last changes fastest.
Arguments:
- modes: bfloat16 [2, 384, 384, 3, 128], P(None, 'gx', 'gz'), may hold values from -6 to 6
- wall_grad: bfloat16 [2, 384, 384, 3, 128], P(None, 'gx', 'gz'), may hold values from -6 to 6
Outputs:
- convective: float32 [128, 128, 128], P('gx', 'gz')
All inputs are finite; a program needn't handle non-finite values.
Results may differ from a plain program's by a relative error of at most 0.0038.
Values may be sent and summed in bfloat16 or wider, within the bound.
A program may use at most 64 MiB of HBM per device.

v0:
```python
import math

import jax
import jax.numpy as jnp
from jax import lax
from jax.sharding import PartitionSpec as P

M = 128


def padded_2(block, sides, width):
    for axis, dim in sides:
        count = lax.axis_size(axis)
        forward = [(i, i + 1) for i in range(count - 1)]
        forward.append((count - 1, 0))
        backward = [(target, source) for source, target in forward]
        low = lax.ppermute(
            lax.slice_in_dim(block, block.shape[dim] - width, None, axis=dim), axis, forward
        )
        high = lax.ppermute(lax.slice_in_dim(block, 0, width, axis=dim), axis, backward)
        block = jnp.concatenate([low, block, high], axis=dim)
    return block


def derive_local(padded, axis, cells_x, cells_z):
    coefs = (0.75, -0.15, 1.0 / 60.0)
    total = jnp.zeros(padded[:, 3 : 3 + cells_x, 3 : 3 + cells_z].shape, jnp.float32)
    for shift_by, coef in zip((1, 2, 3), coefs):
        if axis == 1:
            upper = padded[:, 3 + shift_by : 3 + shift_by + cells_x, 3 : 3 + cells_z]
            lower = padded[:, 3 - shift_by : 3 - shift_by + cells_x, 3 : 3 + cells_z]
        else:
            upper = padded[:, 3 : 3 + cells_x, 3 + shift_by : 3 + shift_by + cells_z]
            lower = padded[:, 3 : 3 + cells_x, 3 - shift_by : 3 - shift_by + cells_z]
        total = total + coef * (upper - lower)
    return total


def per_device(modes, wall_grad):
    planes, cells_x, cells_z = (modes.shape[0], modes.shape[1], modes.shape[2])
    count_x = lax.axis_size("gx")
    count_z = lax.axis_size("gz")
    weight = 1.0 / math.sqrt(planes * cells_x * cells_z * count_x * count_z)
    padded = padded_2(modes, (("gx", 1), ("gz", 2)), 3).astype(jnp.float32)
    points = planes * cells_x * cells_z
    grad_x = derive_local(padded, 1, cells_x, cells_z).astype(jnp.bfloat16).reshape(points, 3, M)
    grad_z = derive_local(padded, 2, cells_x, cells_z).astype(jnp.bfloat16).reshape(points, 3, M)
    grad_y = wall_grad.reshape(points, 3, M)
    flat = modes.reshape(points, 3, M)
    left = flat.reshape(points * 3, M)
    grads = (grad_x, grad_y, grad_z)

    def block_term(k_start, k_count):
        adv = jnp.zeros((points, 3, k_count, M), jnp.float32)
        for comp in range(3):
            part = lax.dynamic_slice_in_dim(grads[comp], k_start, k_count, 2)
            adv = adv + part[:, :, :, None].astype(jnp.float32) * flat[
                :, comp, None, None, :
            ].astype(jnp.float32)
        adv = adv.astype(jnp.bfloat16).reshape(points * 3, k_count * M)
        prod = lax.dot_general(
            left, adv, (((0,), (0,)), ((), ())), preferred_element_type=jnp.float32
        )
        return prod.reshape(M, k_count, M) * weight

    step_size = math.gcd(lax.axis_size("gx") * (M // count_x), 8)

    def one(index):
        term = block_term(index * step_size, step_size)
        return jnp.transpose(term, (1, 0, 2))

    pieces = lax.map(
        one, jnp.arange(lax.axis_size("gx") * (M // count_x) // step_size, dtype=jnp.int32)
    )
    slab = lax.psum_scatter(
        pieces.reshape(lax.axis_size("gx") * (M // count_x), M, M),
        "gx",
        scatter_dimension=0,
        tiled=True,
    )
    result = lax.psum_scatter(slab, "gz", scatter_dimension=1, tiled=True)
    return result


def solution(mesh):
    placed = (P(None, "gx", "gz", None, None), P(None, "gx", "gz", None, None))
    return jax.shard_map(
        per_device, mesh=mesh, in_specs=placed, out_specs=P("gx", "gz", None), check_vma=False
    )
```

profile of v0, /device:TPU:24, one launch (start us, length us, event | category | flops | bytes accessed | tf_op | source)
XLA Modules:
  0.0 626.2 jit_solution(13256220735473249506)
XLA Ops:
  9.3 3.5 collective-permute-start.1
  12.8 5.1 collective-permute-done
  19.3 4.9 collective-permute-start.3
  29.7 2.6 fusion.8
  35.6 364.8 %while.10 = (s32[]{:T(128)}, f32[16,8,128,128]{3,2,1,0:T(8,128)}, s32[16]{0:T(128)S(1)}, bf16[1152,3,128]{2,1,0:T(4,128)(2,1)}, bf16[1152,3,128]{2,1,0:T(4,128)(...) while((s32[]{:T(128)}, f32[16,8,128,128]{3,2,1,0:T(8,128)}, ...), condition=%wide.region_1.2_spmd, body=%wide.region_0.1_spmd.sunk | while | flops 927859712 | bytes 26454740 | solution.py:72
  36.7 2.5 dynamic-slice_convert_fusion.5
  42.3 12.9 %add_convert_fusion.2 = bf16[1152,3,8,128]{3,2,1,0:T(8,128)(2,1)S(1)} fusion(f32[1152,128]{1,0:T(8,128)S(1)} %bitcast.43, f32[1152,3,8]{2,1,0:T(4,128)S(1)} %get-tuple-element.130, f32[1152,128]{1,0:T(8,128)S(1)} %bitcast.44, f32[1152,3,8]{2,1,0:T(4,128)S(1)} %get-tuple-element.132, f32[1152,128]{1,0:T(8,128)S(1)} %bitcast.42, ...), kind=kLoop, calls=%fused_computation.clone.1 | loop fusion | flops 21233664 | bytes 9179136 | tf_op jit(solution)/shard_map/while/body/eval_jaxpr/convert_element_type | solution.py:60
  55.2 2.1 fusion.26
  59.5 2.5 dynamic-slice_convert_fusion.5
  65.1 12.9 %add_convert_fusion.2 = bf16[1152,3,8,128]{3,2,1,0:T(8,128)(2,1)S(1)} fusion(f32[1152,128]{1,0:T(8,128)S(1)} %bitcast.43, f32[1152,3,8]{2,1,0:T(4,128)S(1)} %get-tuple-element.130, f32[1152,128]{1,0:T(8,128)S(1)} %bitcast.44, f32[1152,3,8]{2,1,0:T(4,128)S(1)} %get-tuple-element.132, f32[1152,128]{1,0:T(8,128)S(1)} %bitcast.42, ...), kind=kLoop, calls=%fused_computation.clone.1 | loop fusion | flops 21233664 | bytes 9179136 | tf_op jit(solution)/shard_map/while/body/eval_jaxpr/convert_element_type | solution.py:60
  82.3 2.5 dynamic-slice_convert_fusion.5
  87.9 12.9 %add_convert_fusion.2 = bf16[1152,3,8,128]{3,2,1,0:T(8,128)(2,1)S(1)} fusion(f32[1152,128]{1,0:T(8,128)S(1)} %bitcast.43, f32[1152,3,8]{2,1,0:T(4,128)S(1)} %get-tuple-element.130, f32[1152,128]{1,0:T(8,128)S(1)} %bitcast.44, f32[1152,3,8]{2,1,0:T(4,128)S(1)} %get-tuple-element.132, f32[1152,128]{1,0:T(8,128)S(1)} %bitcast.42, ...), kind=kLoop, calls=%fused_computation.clone.1 | loop fusion | flops 21233664 | bytes 9179136 | tf_op jit(solution)/shard_map/while/body/eval_jaxpr/convert_element_type | solution.py:60
  105.1 2.5 dynamic-slice_convert_fusion.5
  110.7 12.9 %add_convert_fusion.2 = bf16[1152,3,8,128]{3,2,1,0:T(8,128)(2,1)S(1)} fusion(f32[1152,128]{1,0:T(8,128)S(1)} %bitcast.43, f32[1152,3,8]{2,1,0:T(4,128)S(1)} %get-tuple-element.130, f32[1152,128]{1,0:T(8,128)S(1)} %bitcast.44, f32[1152,3,8]{2,1,0:T(4,128)S(1)} %get-tuple-element.132, f32[1152,128]{1,0:T(8,128)S(1)} %bitcast.42, ...), kind=kLoop, calls=%fused_computation.clone.1 | loop fusion | flops 21233664 | bytes 9179136 | tf_op jit(solution)/shard_map/while/body/eval_jaxpr/convert_element_type | solution.py:60
  123.6 2.1 fusion.26
  127.9 2.5 dynamic-slice_convert_fusion.5
  133.5 12.9 %add_convert_fusion.2 = bf16[1152,3,8,128]{3,2,1,0:T(8,128)(2,1)S(1)} fusion(f32[1152,128]{1,0:T(8,128)S(1)} %bitcast.43, f32[1152,3,8]{2,1,0:T(4,128)S(1)} %get-tuple-element.130, f32[1152,128]{1,0:T(8,128)S(1)} %bitcast.44, f32[1152,3,8]{2,1,0:T(4,128)S(1)} %get-tuple-element.132, f32[1152,128]{1,0:T(8,128)S(1)} %bitcast.42, ...), kind=kLoop, calls=%fused_computation.clone.1 | loop fusion | flops 21233664 | bytes 9179136 | tf_op jit(solution)/shard_map/while/body/eval_jaxpr/convert_element_type | solution.py:60
  150.7 2.5 dynamic-slice_convert_fusion.5
  156.3 12.9 %add_convert_fusion.2 = bf16[1152,3,8,128]{3,2,1,0:T(8,128)(2,1)S(1)} fusion(f32[1152,128]{1,0:T(8,128)S(1)} %bitcast.43, f32[1152,3,8]{2,1,0:T(4,128)S(1)} %get-tuple-element.130, f32[1152,128]{1,0:T(8,128)S(1)} %bitcast.44, f32[1152,3,8]{2,1,0:T(4,128)S(1)} %get-tuple-element.132, f32[1152,128]{1,0:T(8,128)S(1)} %bitcast.42, ...), kind=kLoop, calls=%fused_computation.clone.1 | loop fusion | flops 21233664 | bytes 9179136 | tf_op jit(solution)/shard_map/while/body/eval_jaxpr/convert_element_type | solution.py:60
  169.2 2.1 fusion.26
  173.5 2.5 dynamic-slice_convert_fusion.5
  179.1 12.9 %add_convert_fusion.2 = bf16[1152,3,8,128]{3,2,1,0:T(8,128)(2,1)S(1)} fusion(f32[1152,128]{1,0:T(8,128)S(1)} %bitcast.43, f32[1152,3,8]{2,1,0:T(4,128)S(1)} %get-tuple-element.130, f32[1152,128]{1,0:T(8,128)S(1)} %bitcast.44, f32[1152,3,8]{2,1,0:T(4,128)S(1)} %get-tuple-element.132, f32[1152,128]{1,0:T(8,128)S(1)} %bitcast.42, ...), kind=kLoop, calls=%fused_computation.clone.1 | loop fusion | flops 21233664 | bytes 9179136 | tf_op jit(solution)/shard_map/while/body/eval_jaxpr/convert_element_type | solution.py:60
  192.0 2.1 fusion.26
  196.3 2.5 dynamic-slice_convert_fusion.5
  201.9 12.9 %add_convert_fusion.2 = bf16[1152,3,8,128]{3,2,1,0:T(8,128)(2,1)S(1)} fusion(f32[1152,128]{1,0:T(8,128)S(1)} %bitcast.43, f32[1152,3,8]{2,1,0:T(4,128)S(1)} %get-tuple-element.130, f32[1152,128]{1,0:T(8,128)S(1)} %bitcast.44, f32[1152,3,8]{2,1,0:T(4,128)S(1)} %get-tuple-element.132, f32[1152,128]{1,0:T(8,128)S(1)} %bitcast.42, ...), kind=kLoop, calls=%fused_computation.clone.1 | loop fusion | flops 21233664 | bytes 9179136 | tf_op jit(solution)/shard_map/while/body/eval_jaxpr/convert_element_type | solution.py:60
  214.8 2.1 fusion.26
  219.1 2.5 dynamic-slice_convert_fusion.5
  224.7 12.9 %add_convert_fusion.2 = bf16[1152,3,8,128]{3,2,1,0:T(8,128)(2,1)S(1)} fusion(f32[1152,128]{1,0:T(8,128)S(1)} %bitcast.43, f32[1152,3,8]{2,1,0:T(4,128)S(1)} %get-tuple-element.130, f32[1152,128]{1,0:T(8,128)S(1)} %bitcast.44, f32[1152,3,8]{2,1,0:T(4,128)S(1)} %get-tuple-element.132, f32[1152,128]{1,0:T(8,128)S(1)} %bitcast.42, ...), kind=kLoop, calls=%fused_computation.clone.1 | loop fusion | flops 21233664 | bytes 9179136 | tf_op jit(solution)/shard_map/while/body/eval_jaxpr/convert_element_type | solution.py:60
  237.6 2.1 fusion.26
  241.9 2.5 dynamic-slice_convert_fusion.5
  247.5 12.9 %add_convert_fusion.2 = bf16[1152,3,8,128]{3,2,1,0:T(8,128)(2,1)S(1)} fusion(f32[1152,128]{1,0:T(8,128)S(1)} %bitcast.43, f32[1152,3,8]{2,1,0:T(4,128)S(1)} %get-tuple-element.130, f32[1152,128]{1,0:T(8,128)S(1)} %bitcast.44, f32[1152,3,8]{2,1,0:T(4,128)S(1)} %get-tuple-element.132, f32[1152,128]{1,0:T(8,128)S(1)} %bitcast.42, ...), kind=kLoop, calls=%fused_computation.clone.1 | loop fusion | flops 21233664 | bytes 9179136 | tf_op jit(solution)/shard_map/while/body/eval_jaxpr/convert_element_type | solution.py:60
  264.7 2.5 dynamic-slice_convert_fusion.5
  270.3 12.9 %add_convert_fusion.2 = bf16[1152,3,8,128]{3,2,1,0:T(8,128)(2,1)S(1)} fusion(f32[1152,128]{1,0:T(8,128)S(1)} %bitcast.43, f32[1152,3,8]{2,1,0:T(4,128)S(1)} %get-tuple-element.130, f32[1152,128]{1,0:T(8,128)S(1)} %bitcast.44, f32[1152,3,8]{2,1,0:T(4,128)S(1)} %get-tuple-element.132, f32[1152,128]{1,0:T(8,128)S(1)} %bitcast.42, ...), kind=kLoop, calls=%fused_computation.clone.1 | loop fusion | flops 21233664 | bytes 9179136 | tf_op jit(solution)/shard_map/while/body/eval_jaxpr/convert_element_type | solution.py:60
  283.2 2.1 fusion.26
  287.5 2.5 dynamic-slice_convert_fusion.5
  293.1 12.9 %add_convert_fusion.2 = bf16[1152,3,8,128]{3,2,1,0:T(8,128)(2,1)S(1)} fusion(f32[1152,128]{1,0:T(8,128)S(1)} %bitcast.43, f32[1152,3,8]{2,1,0:T(4,128)S(1)} %get-tuple-element.130, f32[1152,128]{1,0:T(8,128)S(1)} %bitcast.44, f32[1152,3,8]{2,1,0:T(4,128)S(1)} %get-tuple-element.132, f32[1152,128]{1,0:T(8,128)S(1)} %bitcast.42, ...), kind=kLoop, calls=%fused_computation.clone.1 | loop fusion | flops 21233664 | bytes 9179136 | tf_op jit(solution)/shard_map/while/body/eval_jaxpr/convert_element_type | solution.py:60
  310.3 2.5 dynamic-slice_convert_fusion.5
  315.9 12.9 %add_convert_fusion.2 = bf16[1152,3,8,128]{3,2,1,0:T(8,128)(2,1)S(1)} fusion(f32[1152,128]{1,0:T(8,128)S(1)} %bitcast.43, f32[1152,3,8]{2,1,0:T(4,128)S(1)} %get-tuple-element.130, f32[1152,128]{1,0:T(8,128)S(1)} %bitcast.44, f32[1152,3,8]{2,1,0:T(4,128)S(1)} %get-tuple-element.132, f32[1152,128]{1,0:T(8,128)S(1)} %bitcast.42, ...), kind=kLoop, calls=%fused_computation.clone.1 | loop fusion | flops 21233664 | bytes 9179136 | tf_op jit(solution)/shard_map/while/body/eval_jaxpr/convert_element_type | solution.py:60
  333.1 2.5 dynamic-slice_convert_fusion.5
  338.7 12.9 %add_convert_fusion.2 = bf16[1152,3,8,128]{3,2,1,0:T(8,128)(2,1)S(1)} fusion(f32[1152,128]{1,0:T(8,128)S(1)} %bitcast.43, f32[1152,3,8]{2,1,0:T(4,128)S(1)} %get-tuple-element.130, f32[1152,128]{1,0:T(8,128)S(1)} %bitcast.44, f32[1152,3,8]{2,1,0:T(4,128)S(1)} %get-tuple-element.132, f32[1152,128]{1,0:T(8,128)S(1)} %bitcast.42, ...), kind=kLoop, calls=%fused_computation.clone.1 | loop fusion | flops 21233664 | bytes 9179136 | tf_op jit(solution)/shard_map/while/body/eval_jaxpr/convert_element_type | solution.py:60
  355.9 2.5 dynamic-slice_convert_fusion.5
  361.5 12.9 %add_convert_fusion.2 = bf16[1152,3,8,128]{3,2,1,0:T(8,128)(2,1)S(1)} fusion(f32[1152,128]{1,0:T(8,128)S(1)} %bitcast.43, f32[1152,3,8]{2,1,0:T(4,128)S(1)} %get-tuple-element.130, f32[1152,128]{1,0:T(8,128)S(1)} %bitcast.44, f32[1152,3,8]{2,1,0:T(4,128)S(1)} %get-tuple-element.132, f32[1152,128]{1,0:T(8,128)S(1)} %bitcast.42, ...), kind=kLoop, calls=%fused_computation.clone.1 | loop fusion | flops 21233664 | bytes 9179136 | tf_op jit(solution)/shard_map/while/body/eval_jaxpr/convert_element_type | solution.py:60
  374.4 2.1 fusion.26
  378.7 2.5 dynamic-slice_convert_fusion.5
  384.3 12.9 %add_convert_fusion.2 = bf16[1152,3,8,128]{3,2,1,0:T(8,128)(2,1)S(1)} fusion(f32[1152,128]{1,0:T(8,128)S(1)} %bitcast.43, f32[1152,3,8]{2,1,0:T(4,128)S(1)} %get-tuple-element.130, f32[1152,128]{1,0:T(8,128)S(1)} %bitcast.44, f32[1152,3,8]{2,1,0:T(4,128)S(1)} %get-tuple-element.132, f32[1152,128]{1,0:T(8,128)S(1)} %bitcast.42, ...), kind=kLoop, calls=%fused_computation.clone.1 | loop fusion | flops 21233664 | bytes 9179136 | tf_op jit(solution)/shard_map/while/body/eval_jaxpr/convert_element_type | solution.py:60
  397.2 2.1 fusion.26
  400.4 168.3 %reduce-scatter.3.cloned.1.call-done = f32[4,128,128]{2,1,0:T(8,128)} async-done(((f32[128,128,128]{2,1,0:T(8,128)}), f32[4,128,128]{2,1,0:T(8,128)}) %reduce-scatter.3.cloned.1.call-update) | async-done | bytes 262160 | tf_op jit(solution)/shard_map/reduce_scatter | solution.py:75
  568.8 50.6 %reduce-scatter.5.cloned.1.call-done = f32[4,16,128]{2,1,0:T(8,128)} async-done(((f32[4,128,128]{2,1,0:T(8,128)}), f32[4,16,128]{2,1,0:T(8,128)}) %reduce-scatter.5.cloned.1.call-update) | async-done | bytes 32784 | tf_op jit(solution)/shard_map/reduce_scatter | solution.py:81
  (147 shorter events, 103.2 us)
Async XLA Ops:
  6.5 11.4 %copy-start = (bf16[2,12,48,3,128]{4,2,3,1,0:T(8,128)(2,1)S(1)}, bf16[2,12,48,3,128]{4,2,3,1,0:T(8,128)(2,1)}, u32[]{:S(2)}) copy-start(bf16[2,12,48,3,128]{4,2,3,1,0:T(8,128)(2,1)} %param.4) | copy-start | bytes 2654212
  6.5 562.2 %reduce-scatter.3.cloned.1.call-start = ((), (), s32[]{:S(2)}) async-start(), calls=%async_computation.2 | async-start | bytes 8650752 | tf_op jit(solution)/shard_map/reduce_scatter | solution.py:75
  7.7 10.3 %collective-permute-start = (bf16[2,3,48,3,128]{4,2,3,1,0:T(8,128)(2,1)S(1)}, bf16[2,3,48,3,128]{4,2,3,1,0:T(8,128)(2,1)S(1)}, u32[]{:S(2)}, u32[]{:S(2)}) collective-permute-start(bf16[2,3,48,3,128]{4,2,3,1,0:T(8,128)(2,1)S(1)} %get-tuple-element.74), channel_id=1, source_target_pairs={{0,8},{8,16},{16,24},{24,32},{32,40},{40,48},{48,56},{56,64},{64,7... | collective-permute-start | bytes 663560 | tf_op jit(solution)/shard_map/ppermute | solution.py:17
  9.3 8.8 %collective-permute-start.1 = (bf16[2,3,48,3,128]{4,2,3,1,0:T(8,128)(2,1)S(1)}, bf16[2,3,48,3,128]{4,2,3,1,0:T(8,128)(2,1)S(1)}, u32[]{:S(2)}, u32[]{:S(2)}) collective-permute-start(bf16[2,3,48,3,128]{4,2,3,1,0:T(8,128)(2,1)S(1)} %get-tuple-element.73), channel_id=1, source_target_pairs={{8,0},{16,8},{24,16},{32,24},{40,32},{48,40},{56,48},{64,56},{72,6... | collective-permute-start | bytes 663560 | tf_op jit(solution)/shard_map/ppermute | solution.py:20
  18.2 1.1 copy-start.1
  18.3 9.0 %collective-permute-start.2 = (bf16[2,18,3,3,128]{4,2,3,1,0:T(4,128)(2,1)S(1)}, bf16[2,18,3,3,128]{4,2,3,1,0:T(4,128)(2,1)}, u32[]{:S(2)}, u32[]{:S(2)}) collective-permute-start(bf16[2,18,3,3,128]{4,2,3,1,0:T(4,128)(2,1)S(1)} %get-tuple-element.71), channel_id=1, source_target_pairs={{0,1},{1,2},{2,3},{3,4},{4,5},{5,6},{6,7},{7,0},{8,9},{9,10},{10,1... | collective-permute-start | bytes 248840 | tf_op jit(solution)/shard_map/ppermute | solution.py:17
  19.3 7.4 %copy-start.2 = (bf16[2,12,48,3,128]{4,2,3,1,0:T(8,128)(2,1)S(1)}, bf16[2,12,48,3,128]{4,2,3,1,0:T(8,128)(2,1)}, u32[]{:S(2)}) copy-start(bf16[2,12,48,3,128]{4,2,3,1,0:T(8,128)(2,1)} %param.5) | copy-start | bytes 2654212
  19.3 8.3 %collective-permute-start.3 = (bf16[2,18,3,3,128]{4,2,3,1,0:T(4,128)(2,1)S(1)}, bf16[2,18,3,3,128]{4,2,3,1,0:T(4,128)(2,1)}, u32[]{:S(2)}, u32[]{:S(2)}) collective-permute-start(bf16[2,18,3,3,128]{4,2,3,1,0:T(4,128)(2,1)S(1)} %get-tuple-element.72), channel_id=1, source_target_pairs={{1,0},{2,1},{3,2},{4,3},{5,4},{6,5},{7,6},{0,7},{9,8},{10,9},{11,1... | collective-permute-start | bytes 248840 | tf_op jit(solution)/shard_map/ppermute | solution.py:20
  42.3 12.9 %copy-start.3 = (bf16[3456,128]{1,0:T(8,128)(2,1)S(1)}, bf16[3456,128]{1,0:T(8,128)(2,1)}, u32[]{:S(2)}) copy-start(bf16[3456,128]{1,0:T(8,128)(2,1)} %get-tuple-element.165) | copy-start | bytes 2654212 | tf_op jit(solution)/shard_map/while
  65.1 12.9 %copy-start.3 = (bf16[3456,128]{1,0:T(8,128)(2,1)S(1)}, bf16[3456,128]{1,0:T(8,128)(2,1)}, u32[]{:S(2)}) copy-start(bf16[3456,128]{1,0:T(8,128)(2,1)} %get-tuple-element.165) | copy-start | bytes 2654212 | tf_op jit(solution)/shard_map/while
  87.9 12.9 %copy-start.3 = (bf16[3456,128]{1,0:T(8,128)(2,1)S(1)}, bf16[3456,128]{1,0:T(8,128)(2,1)}, u32[]{:S(2)}) copy-start(bf16[3456,128]{1,0:T(8,128)(2,1)} %get-tuple-element.165) | copy-start | bytes 2654212 | tf_op jit(solution)/shard_map/while
  110.7 12.9 %copy-start.3 = (bf16[3456,128]{1,0:T(8,128)(2,1)S(1)}, bf16[3456,128]{1,0:T(8,128)(2,1)}, u32[]{:S(2)}) copy-start(bf16[3456,128]{1,0:T(8,128)(2,1)} %get-tuple-element.165) | copy-start | bytes 2654212 | tf_op jit(solution)/shard_map/while
  133.5 12.9 %copy-start.3 = (bf16[3456,128]{1,0:T(8,128)(2,1)S(1)}, bf16[3456,128]{1,0:T(8,128)(2,1)}, u32[]{:S(2)}) copy-start(bf16[3456,128]{1,0:T(8,128)(2,1)} %get-tuple-element.165) | copy-start | bytes 2654212 | tf_op jit(solution)/shard_map/while
  156.3 12.9 %copy-start.3 = (bf16[3456,128]{1,0:T(8,128)(2,1)S(1)}, bf16[3456,128]{1,0:T(8,128)(2,1)}, u32[]{:S(2)}) copy-start(bf16[3456,128]{1,0:T(8,128)(2,1)} %get-tuple-element.165) | copy-start | bytes 2654212 | tf_op jit(solution)/shard_map/while
  179.1 12.9 %copy-start.3 = (bf16[3456,128]{1,0:T(8,128)(2,1)S(1)}, bf16[3456,128]{1,0:T(8,128)(2,1)}, u32[]{:S(2)}) copy-start(bf16[3456,128]{1,0:T(8,128)(2,1)} %get-tuple-element.165) | copy-start | bytes 2654212 | tf_op jit(solution)/shard_map/while
  201.9 12.9 %copy-start.3 = (bf16[3456,128]{1,0:T(8,128)(2,1)S(1)}, bf16[3456,128]{1,0:T(8,128)(2,1)}, u32[]{:S(2)}) copy-start(bf16[3456,128]{1,0:T(8,128)(2,1)} %get-tuple-element.165) | copy-start | bytes 2654212 | tf_op jit(solution)/shard_map/while
  224.7 12.9 %copy-start.3 = (bf16[3456,128]{1,0:T(8,128)(2,1)S(1)}, bf16[3456,128]{1,0:T(8,128)(2,1)}, u32[]{:S(2)}) copy-start(bf16[3456,128]{1,0:T(8,128)(2,1)} %get-tuple-element.165) | copy-start | bytes 2654212 | tf_op jit(solution)/shard_map/while
  247.5 12.9 %copy-start.3 = (bf16[3456,128]{1,0:T(8,128)(2,1)S(1)}, bf16[3456,128]{1,0:T(8,128)(2,1)}, u32[]{:S(2)}) copy-start(bf16[3456,128]{1,0:T(8,128)(2,1)} %get-tuple-element.165) | copy-start | bytes 2654212 | tf_op jit(solution)/shard_map/while
  270.3 12.9 %copy-start.3 = (bf16[3456,128]{1,0:T(8,128)(2,1)S(1)}, bf16[3456,128]{1,0:T(8,128)(2,1)}, u32[]{:S(2)}) copy-start(bf16[3456,128]{1,0:T(8,128)(2,1)} %get-tuple-element.165) | copy-start | bytes 2654212 | tf_op jit(solution)/shard_map/while
  293.1 12.9 %copy-start.3 = (bf16[3456,128]{1,0:T(8,128)(2,1)S(1)}, bf16[3456,128]{1,0:T(8,128)(2,1)}, u32[]{:S(2)}) copy-start(bf16[3456,128]{1,0:T(8,128)(2,1)} %get-tuple-element.165) | copy-start | bytes 2654212 | tf_op jit(solution)/shard_map/while
  315.9 12.9 %copy-start.3 = (bf16[3456,128]{1,0:T(8,128)(2,1)S(1)}, bf16[3456,128]{1,0:T(8,128)(2,1)}, u32[]{:S(2)}) copy-start(bf16[3456,128]{1,0:T(8,128)(2,1)} %get-tuple-element.165) | copy-start | bytes 2654212 | tf_op jit(solution)/shard_map/while
  338.7 12.9 %copy-start.3 = (bf16[3456,128]{1,0:T(8,128)(2,1)S(1)}, bf16[3456,128]{1,0:T(8,128)(2,1)}, u32[]{:S(2)}) copy-start(bf16[3456,128]{1,0:T(8,128)(2,1)} %get-tuple-element.165) | copy-start | bytes 2654212 | tf_op jit(solution)/shard_map/while
  361.5 12.9 %copy-start.3 = (bf16[3456,128]{1,0:T(8,128)(2,1)S(1)}, bf16[3456,128]{1,0:T(8,128)(2,1)}, u32[]{:S(2)}) copy-start(bf16[3456,128]{1,0:T(8,128)(2,1)} %get-tuple-element.165) | copy-start | bytes 2654212 | tf_op jit(solution)/shard_map/while
  384.3 12.9 %copy-start.3 = (bf16[3456,128]{1,0:T(8,128)(2,1)S(1)}, bf16[3456,128]{1,0:T(8,128)(2,1)}, u32[]{:S(2)}) copy-start(bf16[3456,128]{1,0:T(8,128)(2,1)} %get-tuple-element.165) | copy-start | bytes 2654212 | tf_op jit(solution)/shard_map/while
  400.4 219.0 %reduce-scatter.5.cloned.1.call-start = ((), (), s32[]{:S(2)}) async-start(), calls=%async_computation.3 | async-start | bytes 294912 | tf_op jit(solution)/shard_map/reduce_scatter | solution.py:81
Sparse Core Ops, SparseCore 0:
  400.5 168.1 reduce-scatter.2
  571.2 48.0 reduce-scatter.4
where the time goes:
time: 627 us; the launch traced here: 626 us
  other arithmetic  300 us (48%)
  waiting for transfers between devices  224 us (36%)
  local copies, waits for them, and re-layouts  34.7 us (6%)
  matrix products  33.3 us (5%)
  between operations  13.5 us (2%)
  loops' own time  10.2 us (2%)
  starting transfers between devices  10.1 us (2%)
    convert_element_type x16, other arithmetic, block_term(): adv = adv.astype(jnp.bfloat16).reshape(points * 3, k_count * M)  206 us
    reduce_scatter x1, waiting for transfers between devices, per_device(): lax.psum_scatter(pieces.reshape(lax.axis_size('gx') * (M // count_x), M,...  168 us
    convert_element_type x32, other arithmetic, block_term(): part[:, :, :, None].astype(jnp.float32)  68.9 us
    reduce_scatter x1, waiting for transfers between devices, per_device(): result = lax.psum_scatter(slab, 'gz', scatter_dimension=1, tiled=True)  50.6 us
    dot_general x16, matrix products, block_term(): lax.dot_general(left, adv, (((0,), (0,)), ((), ())), preferred_element_ty...  33.3 us
    convert_element_type x16, other arithmetic, block_term(): adv = adv + part[:, :, :, None].astype(jnp.float32) * flat[:, comp, None,...  20.2 us
    dynamic_update_slice x32, local copies, waits for them, and re-layouts, per_device(): lax.map(one, jnp.arange(lax.axis_size('gx') * (M // count_x) // step_size...  16.7 us
  transfers between devices with their start and end apart: 6, of which 4 were waited for; matrix products, arithmetic and copies ran while one was open for 1% of the time, Pallas kernels for 0%

commit v1 on v0

v1 whole, which is shorter than its diff:
```python
import functools
import math

import jax
import jax.numpy as jnp
from jax import lax
from jax.experimental import pallas as pl
from jax.experimental.pallas import tpu as pltpu
from jax.sharding import PartitionSpec as P

M = 128
BF = jnp.bfloat16
F32 = jnp.float32
MESH = pl.DeviceIdType.MESH
WEIGHT = 1.0 / math.sqrt(2 * 384 * 384)
POINTS = 1152
PASSES = 16


def kernel(phi, phi5, wall, edges, out,
           xlo, xhi, zlo, zhi, zpad, gnat, phil, gt, own, rchip, xsend, rxy, zsend, rz,
           hs_sem, hr_sem, cs_sem, cr_sem, xs_sem, xr_sem, zs_sem, zr_sem):
    gx = lax.axis_index("gx")
    gz = lax.axis_index("gz")
    yy = gx // 8
    zl = (gx // 4) % 2
    xx = gx % 4
    zh = gz // 2
    core = gz % 2
    partner = (gx, zh * 2 + 1 - core)

    def xy_peer(dx, dy):
        return (((yy + dy) % 4) * 8 + zl * 4 + (xx + dx) % 4, gz)

    def z_peer(dz, zr):
        return (yy * 8 + ((zl + zr) % 2) * 4 + xx, ((zh + dz) % 4) * 2 + core)

    x_next = ((gx + 1) % 32, gz)
    x_prev = ((gx + 31) % 32, gz)
    z_next = (gx, (gz + 1) % 8)
    z_prev = (gx, (gz + 7) % 8)

    barrier = pltpu.get_barrier_semaphore()
    peers = [partner, x_next, x_prev, z_next, z_prev]
    peers += [xy_peer(d % 4, d // 4) for d in range(1, 16)]
    peers += [z_peer(d % 4, d // 4) for d in range(1, 8)]
    for peer in peers:
        pl.semaphore_signal(barrier, inc=1, device_id=peer, device_id_type=MESH)
    pl.semaphore_wait(barrier, len(peers))

    def remote(src, dst, ss, rs, dev):
        return pltpu.make_async_remote_copy(
            src_ref=src, dst_ref=dst, send_sem=ss, recv_sem=rs, device_id=dev, device_id_type=MESH)

    halos = [
        remote(phi5.at[:, :, 9:12], xlo, hs_sem.at[0], hr_sem.at[0], x_next),
        remote(phi5.at[:, :, 0:3], xhi, hs_sem.at[1], hr_sem.at[1], x_prev),
        remote(edges.at[1], zlo, hs_sem.at[2], hr_sem.at[2], z_next),
        remote(edges.at[0], zhi, hs_sem.at[3], hr_sem.at[3], z_prev),
    ]
    for h in halos:
        h.start()

    zero = jnp.zeros((128, 128), F32)
    for c in range(3):
        for b in range(4):
            for h in range(2):
                rows = slice(b * 256 + h * 128, b * 256 + h * 128 + 128)
                phil[b, c, :, h * 128:h * 128 + 128] = phi[c, rows, :].astype(F32).T.astype(BF)
                gt[3 * b + 1, c, :, h * 128:h * 128 + 128] = wall[c, rows, :].astype(F32).T
        tail = phi[c, 1024:1152, :].astype(F32).T.astype(BF)
        phil[4, c, :, 0:128] = tail
        phil[4, c, :, 128:256] = tail
        gt[12, c, :, 128:256] = wall[c, 1024:1152, :].astype(F32).T
        gt[13, c, :, 128:256] = zero

    def fill(s, carry):
        c, p = s // 2, s % 2
        for x in range(12):
            zpad[s * 12 + x, 8:56, :] = phi5[c, p, x].astype(F32)
        return carry

    lax.fori_loop(0, 6, fill, 0)

    for h in halos:
        h.wait()
    for r in range(3):
        zpad[:, 5 + r, :] = zlo[r, 0:72, :].astype(F32)
        zpad[:, 56 + r, :] = zhi[r, 0:72, :].astype(F32)

    coefs = (0.75, -0.15, 1.0 / 60.0)

    def grads(s, carry):
        c, p = s // 2, s % 2

        def at(x):
            if x < 0:
                return xlo[c, p, x + 3].astype(F32)
            if x >= 12:
                return xhi[c, p, x - 12].astype(F32)
            return phi5[c, p, x].astype(F32)

        for x in range(12):
            total = jnp.zeros((48, M), F32)
            for d, coef in zip((1, 2, 3), coefs):
                total = total + coef * (at(x + d) - at(x - d))
            gnat[0, c, pl.ds(p * 576 + x * 48, 48), :] = total.astype(BF)
            total = jnp.zeros((48, M), F32)
            for d, coef in zip((1, 2, 3), coefs):
                total = total + coef * (
                    zpad[s * 12 + x, 8 + d:56 + d, :] - zpad[s * 12 + x, 8 - d:56 - d, :])
            gnat[1, c, pl.ds(p * 576 + x * 48, 48), :] = total.astype(BF)
        return carry

    lax.fori_loop(0, 6, grads, 0)

    for c in range(3):
        for b in range(4):
            for h in range(2):
                rows = slice(b * 256 + h * 128, b * 256 + h * 128 + 128)
                for n, a in ((0, 0), (1, 2)):
                    gt[3 * b + a, c, :, h * 128:h * 128 + 128] = gnat[n, c, rows, :].astype(F32).T
        gt[12, c, :, 0:128] = gnat[0, c, 1024:1152, :].astype(F32).T
        gt[13, c, :, 0:128] = gnat[1, c, 1024:1152, :].astype(F32).T

    def offsets(half, e):
        dy = e // 2
        return 2 * (e % 2) + (dy + 1 + half) % 2, dy

    def chip_copy(n):
        return remote(own.at[n, :, 1 - core], rchip.at[n], cs_sem.at[n], cr_sem.at[n], partner)

    def xy_copy(n, e):
        dx, dy = offsets(n % 2, e)
        return remote(xsend.at[n, e], rxy.at[n, e], xs_sem.at[n, e], xr_sem.at[n, e], xy_peer(dx, dy))

    def z_copy(q, dz):
        zr, kk = q // 4, q % 4
        return remote(zsend.at[q, (zh + dz) % 4], rz.at[kk, zr * 4 + dz],
                      zs_sem.at[q, dz], zr_sem.at[q, dz], z_peer(dz, zr))

    def send_xy(n):
        chip_copy(n).wait_recv()
        for e in range(8):
            xsend[n, e] = (own[n, e, core] + rchip[n, e]).astype(BF)
        for e in range(8):
            if e:
                xy_copy(n, e).start()
            else:
                @pl.when(n % 2 == 0)
                def _():
                    xy_copy(n, 0).start()

                @pl.when(n % 2 == 1)
                def _():
                    rxy[n, 0] = xsend[n, 0]

    def send_z(q):
        for half in range(2):
            for e in range(half, 8):
                xy_copy(2 * q + half, e).wait_recv()
        for s in range(4):
            total = jnp.zeros((16, M), F32)
            for half in range(2):
                for e in range(8):
                    total = total + rxy[2 * q + half, e, s * 16:s * 16 + 16, :].astype(F32)
            zsend[q, s] = total
        zr, kk = q // 4, q % 4
        for dz in range(1, 4):
            z_copy(q, dz).start()

        @pl.when(zr == 1)
        def _():
            z_copy(q, 0).start()

        @pl.when(zr == 0)
        def _():
            rz[kk, 0] = zsend[q, zh]

    def compute(n):
        q, half = n // 2, n % 2
        zr, kk = q // 4, q % 4
        ks = []
        for e in range(8):
            dx, dy = offsets(half, e)
            ks.append(((yy + dy) % 4) * 32 + ((zl + zr) % 2) * 16 + ((xx + dx) % 4) * 4 + kk)

        def scoped(*accs):
            pad = jnp.zeros((256, M), BF)
            for t in range(14):
                if t < 12:
                    a, b = t % 3, t // 3
                    block = phi[a, b * 256:b * 256 + 256, :]
                    left = b
                elif t == 12:
                    block = jnp.concatenate([phi[0, 1024:1152, :], phi[1, 1024:1152, :]], axis=0)
                    left = 4
                else:
                    block = jnp.concatenate([phi[2, 1024:1152, :], jnp.zeros((128, M), BF)], axis=0)
                    left = 4
                block = jnp.concatenate([block, pad], axis=1)
                for m in (0, 1):
                    pltpu.matmul_push_rhs(block, 0, m)
                ph = [phil[left, c] for c in range(3)]
                for kk4 in range(4):
                    for m in (0, 1):
                        e = m * 4 + kk4
                        rows = []
                        for c in range(3):
                            row = jnp.broadcast_to(gt[t, c, pl.ds(ks[e], 1), :], (8, 256)).astype(BF)
                            rows.append(jnp.concatenate([row] * 16, axis=0))
                        term = ph[0] * rows[0] + ph[1] * rows[1] + ph[2] * rows[2]
                        pltpu.matmul_acc_lhs(accs[e], term, load_staged_rhs=0 if kk4 == 0 else None)
            for e in range(8):
                res = pltpu.matmul_pop(accs[e])
                for s in range(8):
                    own[n, e, s % 2, (s // 2) * 16:(s // 2) * 16 + 16, :] = res[s * 16:s * 16 + 16, :M]

        pl.run_scoped(scoped, *[pltpu.ACC(e // 4)((128, 256), F32) for e in range(8)])
        chip_copy(n).start()

    def step(n, carry):
        compute(n)

        @pl.when(n >= 1)
        def _():
            send_xy(n - 1)

        @pl.when((n >= 3) & (n % 2 == 1))
        def _():
            send_z((n - 3) // 2)

        return carry

    lax.fori_loop(0, PASSES, step, 0)
    send_xy(PASSES - 1)
    send_z(PASSES // 2 - 1)

    for q in range(8):
        for dz in range(0 if q >= 4 else 1, 4):
            z_copy(q, dz).wait_recv()
    for kk in range(4):
        total = rz[kk, 0]
        for s in range(1, 8):
            total = total + rz[kk, s]
        out[kk] = total * WEIGHT

    def drain(n, carry):
        chip_copy(n).wait_send()
        for e in range(1, 8):
            xy_copy(n, e).wait_send()

        @pl.when(n % 2 == 0)
        def _():
            xy_copy(n, 0).wait_send()

        return carry

    lax.fori_loop(0, PASSES, drain, 0)
    for q in range(8):
        for dz in range(0 if q >= 4 else 1, 4):
            z_copy(q, dz).wait_send()


def per_device(modes, wall_grad):
    phi5 = jnp.transpose(modes, (3, 0, 1, 2, 4))
    wall = jnp.transpose(wall_grad, (3, 0, 1, 2, 4)).reshape(3, POINTS, M)
    rows = jnp.stack([modes[:, :, 0:3], modes[:, :, 45:48]])
    edges = jnp.transpose(rows, (0, 3, 4, 1, 2, 5)).reshape(2, 3, 72, M)
    edges = jnp.pad(edges, ((0, 0), (0, 0), (0, 8), (0, 0)))
    vm = pl.BlockSpec(memory_space=pltpu.VMEM)
    dma = pltpu.SemaphoreType.DMA
    return pl.pallas_call(
        kernel,
        out_shape=jax.ShapeDtypeStruct((4, 16, M), F32),
        in_specs=[vm] * 4,
        out_specs=vm,
        scratch_shapes=[
            pltpu.VMEM((3, 2, 3, 48, M), BF),
            pltpu.VMEM((3, 2, 3, 48, M), BF),
            pltpu.VMEM((3, 80, M), BF),
            pltpu.VMEM((3, 80, M), BF),
            pltpu.VMEM((72, 64, M), F32),
            pltpu.VMEM((2, 3, POINTS, M), BF),
            pltpu.VMEM((5, 3, M, 256), BF),
            pltpu.VMEM((14, 3, M, 256), F32),
            pltpu.VMEM((PASSES, 8, 2, 64, M), F32),
            pltpu.VMEM((PASSES, 8, 64, M), F32),
            pltpu.VMEM((PASSES, 8, 64, M), BF),
            pltpu.VMEM((PASSES, 8, 64, M), BF),
            pltpu.VMEM((8, 4, 16, M), F32),
            pltpu.VMEM((4, 8, 16, M), F32),
            dma((4,)), dma((4,)),
            dma((PASSES,)), dma((PASSES,)),
            dma((PASSES, 8)), dma((PASSES, 8)),
            dma((8, 4)), dma((8, 4)),
        ],
        compiler_params=pltpu.CompilerParams(
            collective_id=0, has_side_effects=True, vmem_limit_bytes=56 * 2**20),
        cost_estimate=pl.CostEstimate(
            flops=2 * 128 * 3456 * 16384, bytes_accessed=4 * 2**20, transcendentals=0),
    )(phi5.reshape(3, POINTS, M), phi5, wall, edges)


def solution(mesh):
    placed = (P(None, "gx", "gz", None, None), P(None, "gx", "gz", None, None))
    body = jax.shard_map(
        per_device, mesh=mesh, in_specs=placed, out_specs=P("gx", "gz", None), check_vma=False)

    def run(modes, wall_grad):
        with jax.sharding.use_abstract_mesh(mesh.abstract_mesh):
            return body(modes, wall_grad)

    return run
```

time: 627 us -> 96.1 us (0.15)
  other arithmetic: 300 us -> 0.1 us
  waiting for transfers between devices: 224 us -> 0 us
  Pallas kernels: 0 us -> 88.8 us
  matrix products: 33.3 us -> 0 us
  local copies, waits for them, and re-layouts: 34.7 us -> 5.78 us
  between operations: 13.5 us -> 0.04 us
  loops' own time: 10.2 us -> 0 us
  starting transfers between devices: 10.1 us -> 0 us
    convert_element_type x66 -> x0, other arithmetic: 300 us -> none  [the longest x16 206 us: block_term(): adv = adv.astype(jnp.bfloat16).reshape(points * 3, k_count * M)]
    reduce_scatter x2 -> x0, waiting for transfers between devices: 219 us -> none  [the longest x1 168 us: per_device(): lax.psum_scatter(pieces.reshape(lax.axis_size('gx') * (M // count_x), M,...]
    pallas_call x0 -> x1, Pallas kernels: none -> 88.8 us  [per_device(): pl.pallas_call(kernel, out_shape=jax.ShapeDtypeStruct((4, 16, M), F32), i...]
    dot_general x16 -> x0, matrix products: 33.3 us -> none  [block_term(): lax.dot_general(left, adv, (((0,), (0,)), ((), ())), preferred_element_ty...]
    dynamic_update_slice x32 -> x0, local copies, waits for them, and re-layouts: 16.7 us -> none  [per_device(): lax.map(one, jnp.arange(lax.axis_size('gx') * (M // count_x) // step_size...]
    another operation x1 -> x0, loops' own time: 10.2 us -> none  [per_device(): lax.map(one, jnp.arange(lax.axis_size('gx') * (M // count_x) // step_size...]
    ppermute x4 -> x0, starting transfers between devices: 10.1 us -> none  [the longest x2 8.41 us: padded_2(): lax.ppermute(lax.slice_in_dim(block, 0, width, axis=dim), axis, backward)]
    dynamic_slice x16 -> x0, local copies, waits for them, and re-layouts: 9.15 us -> none  [per_device(): lax.map(one, jnp.arange(lax.axis_size('gx') * (M // count_x) // step_size...]
  transfers between devices with their start and end apart: 6 -> 0, of which waited for: 4 -> 0; matrix products, arithmetic and copies ran while one was open for 1% -> 0% of each run, Pallas kernels for 0% -> 0%
where the time goes in v1:
time: 96.1 us; the launch traced here: 94.7 us
  Pallas kernels  88.8 us (92%)
  local copies, waits for them, and re-layouts  5.78 us (6%)
    pallas_call x1, Pallas kernels, per_device(): pl.pallas_call(kernel, out_shape=jax.ShapeDtypeStruct((4, 16, M), F32), i...  88.8 us
    unnamed x6, local copies, waits for them, and re-layouts  2.87 us

profile of v1, /device:TPU:24, one launch (start us, length us, event | category | flops | bytes accessed | tf_op | source)
XLA Modules:
  0.0 94.7 jit_solution(4181452263659073582)
XLA Ops:
  0.0 0.0 copy-start
  0.0 1.1 %slice_bitcast_fusion.1 = (bf16[1,2,12,3,3,128]{5,3,4,2,1,0:T(4,128)(2,1)S(1)}, bf16[1,2,12,3,3,128]{5,3,4,2,1,0:T(4,128)(2,1)S(1)}) fusion(bf16[2,12,48,3,128]{4,2,3,1,0:T(8,128)(2,1)} %param.2), kind=kLoop, calls=%fused_computation.2 | loop fusion | bytes 221184 | tf_op jit(solution)/shard_map/stack | solution.py:268
  1.1 0.1 maximum_bitcast_fusion
  1.2 0.1 copy.8
  1.4 0.7 pad.4.edges
  2.0 0.0 copy-done
  2.0 0.0 copy-start.1
  2.0 1.0 %copy.12 = bf16[2,12,48,3,128]{4,2,1,0,3:T(8,128)(2,1)} copy(bf16[2,12,48,3,128]{4,2,3,1,0:T(8,128)(2,1)S(1)} %copy-done) | data formatting | bytes 1769472 | tf_op args[0]
  3.0 0.5 copy-done.1
  3.5 1.0 %copy.7 = bf16[3,2,12,48,128]{4,3,2,1,0:T(8,128)(2,1)} copy(bf16[3,2,12,48,128]{4,3,0,2,1:T(8,128)(2,1)S(1)} %bitcast.14) | data formatting | bytes 1769472 | tf_op jit(solution)/shard_map/transpose | solution.py:267
  4.5 88.8 %shard_map.28 = f32[4,16,128]{2,1,0:T(8,128)} custom-call(bf16[3,1152,128]{2,1,0:T(8,128)(2,1)} %bitcast.15, bf16[3,2,12,48,128]{4,3,2,1,0:T(8,128)(2,1)} %bitcast.16, bf16[3,1152,128]{2,1,0:T(8,128)(2,1)} %bitcast.17, bf16[2,3,80,128]{3,2,1,0:T(8,128)(2,1)} %pad.4.edges), custom_call_target="tpu_custom_call" | custom-call | flops 14495514624 | bytes 4194304 | tf_op jit(solution)/shard_map/pallas_call | solution.py:273
  93.4 1.4 %copy.14 = f32[4,16,128]{2,1,0:T(8,128)} copy(f32[4,16,128]{2,1,0:T(8,128)} %shard_map.28) | data formatting | bytes 65536
  (1 shorter events, 0.0 us)
Async XLA Ops:
  0.0 2.0 %copy-start = (bf16[2,12,48,3,128]{4,2,3,1,0:T(8,128)(2,1)S(1)}, bf16[2,12,48,3,128]{4,2,3,1,0:T(8,128)(2,1)}, u32[]{:S(2)}) copy-start(bf16[2,12,48,3,128]{4,2,3,1,0:T(8,128)(2,1)} %param.2) | copy-start | bytes 2654212
  2.0 1.5 %copy-start.1 = (bf16[2,12,48,3,128]{4,2,3,1,0:T(8,128)(2,1)S(1)}, bf16[2,12,48,3,128]{4,2,3,1,0:T(8,128)(2,1)}, u32[]{:S(2)}) copy-start(bf16[2,12,48,3,128]{4,2,3,1,0:T(8,128)(2,1)} %param.3) | copy-start | bytes 2654212

commit v2 on v1

v2 whole, which is shorter than its diff:
```python
import functools
import math

import jax
import jax.numpy as jnp
from jax import lax
from jax.experimental import pallas as pl
from jax.experimental.pallas import tpu as pltpu
from jax.sharding import PartitionSpec as P

M = 128
BF = jnp.bfloat16
F32 = jnp.float32
MESH = pl.DeviceIdType.MESH
WEIGHT = 1.0 / math.sqrt(2 * 384 * 384)
POINTS = 1152
PASSES = 16
EARLY = 5


def kernel(phi, phi5, wall, out,
           edges, xlo, xhi, zlo, zhi, zpad, gnat, phil, gt, own, rchip,
           sa1, sb1, ra1, rb1, sa2, sb2, ra2, rb2, zsend, rz,
           hs_sem, hr_sem, cs_sem, cr_sem, a1s, a1r, b1s, b1r, a2s, a2r, b2s, b2r, zs_sem, zr_sem):
    gx = lax.axis_index("gx")
    gz = lax.axis_index("gz")
    yy = gx // 8
    zl = (gx // 4) % 2
    xx = gx % 4
    zh = gz // 2
    core = gz % 2
    partner = (gx, zh * 2 + 1 - core)

    def x_peer(dx):
        return (yy * 8 + zl * 4 + (xx + dx) % 4, gz)

    def y_peer(dy):
        return (((yy + dy) % 4) * 8 + zl * 4 + xx, gz)

    def z_peer(dz, zr):
        return (yy * 8 + ((zl + zr) % 2) * 4 + xx, ((zh + dz) % 4) * 2 + core)

    x_next = ((gx + 1) % 32, gz)
    x_prev = ((gx + 31) % 32, gz)
    z_next = (gx, (gz + 1) % 8)
    z_prev = (gx, (gz + 7) % 8)

    barrier = pltpu.get_barrier_semaphore()
    peers = [partner, x_next, x_prev, z_next, z_prev]
    peers += [x_peer(d) for d in range(1, 4)] + [y_peer(d) for d in range(1, 4)]
    peers += [z_peer(d % 4, d // 4) for d in range(1, 8)]
    for peer in peers:
        pl.semaphore_signal(barrier, inc=1, device_id=peer, device_id_type=MESH)

    def remote(src, dst, ss, rs, dev):
        return pltpu.make_async_remote_copy(
            src_ref=src, dst_ref=dst, send_sem=ss, recv_sem=rs, device_id=dev, device_id_type=MESH)

    zero = jnp.zeros((M, M), F32)
    for c in range(3):
        for b in range(4):
            for h in range(2):
                rows = slice(b * 256 + h * 128, b * 256 + h * 128 + 128)
                phil[b, c, :, h * 128:h * 128 + 128] = phi[c, rows, :].astype(F32).T.astype(BF)
                gt[b, c, :, h * 128:h * 128 + 128] = wall[c, rows, :].astype(F32).T
        tail = phi[c, 1024:1152, :].astype(F32).T.astype(BF)
        phil[4, c, :, 0:128] = tail
        phil[4, c, :, 128:256] = tail
        gt[4, c, :, 0:128] = wall[c, 1024:1152, :].astype(F32).T
        gt[4, c, :, 128:256] = zero

    def fill(s, carry):
        c, p = s // 2, s % 2
        for x in range(12):
            zpad[s * 12 + x, 8:56, :] = phi5[c, p, x].astype(F32)
        return carry

    lax.fori_loop(0, 6, fill, 0)
    for r in range(3):
        edges[0, r, 0:72, :] = zpad[:, 8 + r, :].astype(BF)
        edges[1, r, 0:72, :] = zpad[:, 53 + r, :].astype(BF)
        for side in range(2):
            edges[side, r, 72:80, :] = jnp.zeros((8, M), BF)

    def modes_of(n):
        q, half = n // 2, n % 2
        zr, kk = q // 4, q % 4
        ks = []
        for e in range(8):
            dx, dy = e % 4, 2 * (e // 4) + 1 - half
            ks.append(((yy + dy) % 4) * 32 + ((zl + zr) % 2) * 16 + ((xx + dx) % 4) * 4 + kk)
        return ks

    def contract(n, tiles, first):
        ks = modes_of(n)

        def scoped(*accs):
            for t, left, parts in tiles:
                block = [phi[a, lo:lo + size, :] for a, lo, size in parts]
                size = sum(p[2] for p in parts)
                if size < 256:
                    block.append(jnp.zeros((256 - size, M), BF))
                block = jnp.concatenate(block, axis=0) if len(block) > 1 else block[0]
                block = jnp.concatenate([block, jnp.zeros((256, M), BF)], axis=1)
                for m in (0, 1):
                    pltpu.matmul_push_rhs(block, 0, m)
                ph = [phil[left, c] for c in range(3)]
                for j in range(4):
                    for m in (0, 1):
                        e = m * 4 + j
                        rows = []
                        for c in range(3):
                            row = jnp.broadcast_to(gt[t, c, pl.ds(ks[e], 1), :], (8, 256)).astype(BF)
                            rows.append(jnp.concatenate([row] * 16, axis=0))
                        term = ph[0] * rows[0] + ph[1] * rows[1] + ph[2] * rows[2]
                        pltpu.matmul_acc_lhs(accs[e], term, load_staged_rhs=0 if j == 0 else None)
            for e in range(8):
                res = pltpu.matmul_pop(accs[e])
                for s in range(8):
                    piece = res[s * 16:s * 16 + 16, :M]
                    spot = slice((s // 2) * 16, (s // 2) * 16 + 16)
                    if not first:
                        piece = piece + own[n, e, s % 2, spot, :]
                    own[n, e, s % 2, spot, :] = piece

        pl.run_scoped(scoped, *[pltpu.ACC(e // 4)((M, 256), F32) for e in range(8)])

    y_tiles = [(b, b, [(1, b * 256, 256)]) for b in range(4)] + [(4, 4, [(1, 1024, 128)])]
    xz_tiles = []
    for b in range(4):
        xz_tiles += [(5 + 2 * b, b, [(0, b * 256, 256)]), (6 + 2 * b, b, [(2, b * 256, 256)])]
    xz_tiles.append((13, 4, [(0, 1024, 128), (2, 1024, 128)]))

    def wall_pass(n, carry):
        contract(n, y_tiles, True)
        return carry

    lax.fori_loop(0, EARLY, wall_pass, 0)
    pl.semaphore_wait(barrier, len(peers))
    halos = [
        remote(phi5.at[:, :, 9:12], xlo, hs_sem.at[0], hr_sem.at[0], x_next),
        remote(phi5.at[:, :, 0:3], xhi, hs_sem.at[1], hr_sem.at[1], x_prev),
        remote(edges.at[1], zlo, hs_sem.at[2], hr_sem.at[2], z_next),
        remote(edges.at[0], zhi, hs_sem.at[3], hr_sem.at[3], z_prev),
    ]
    for h in halos:
        h.start()
    lax.fori_loop(EARLY, PASSES, wall_pass, 0)
    for h in halos:
        h.wait()

    for r in range(3):
        zpad[:, 5 + r, :] = zlo[r, 0:72, :].astype(F32)
        zpad[:, 56 + r, :] = zhi[r, 0:72, :].astype(F32)

    coefs = (0.75, -0.15, 1.0 / 60.0)

    def grads(s, carry):
        c, p = s // 2, s % 2

        def at(x):
            if x < 0:
                return xlo[c, p, x + 3].astype(F32)
            if x >= 12:
                return xhi[c, p, x - 12].astype(F32)
            return phi5[c, p, x].astype(F32)

        for x in range(12):
            total = jnp.zeros((48, M), F32)
            for d, coef in zip((1, 2, 3), coefs):
                total = total + coef * (at(x + d) - at(x - d))
            gnat[0, c, pl.ds(p * 576 + x * 48, 48), :] = total.astype(BF)
            total = jnp.zeros((48, M), F32)
            for d, coef in zip((1, 2, 3), coefs):
                total = total + coef * (
                    zpad[s * 12 + x, 8 + d:56 + d, :] - zpad[s * 12 + x, 8 - d:56 - d, :])
            gnat[1, c, pl.ds(p * 576 + x * 48, 48), :] = total.astype(BF)
        return carry

    lax.fori_loop(0, 6, grads, 0)

    for c in range(3):
        for b in range(4):
            for h in range(2):
                rows = slice(b * 256 + h * 128, b * 256 + h * 128 + 128)
                for a in range(2):
                    gt[5 + 2 * b + a, c, :, h * 128:h * 128 + 128] = gnat[a, c, rows, :].astype(F32).T
        gt[13, c, :, 0:128] = gnat[0, c, 1024:1152, :].astype(F32).T
        gt[13, c, :, 128:256] = gnat[1, c, 1024:1152, :].astype(F32).T

    def chip_copy(n):
        return remote(own.at[n, :, 1 - core], rchip.at[n], cs_sem.at[n], cr_sem.at[n], partner)

    def a1_copy(n, dx):
        return remote(sa1.at[n, dx], ra1.at[n, dx], a1s.at[n, dx], a1r.at[n, dx], x_peer(dx))

    def b1_copy(n, i):
        return remote(sb1.at[n, i], rb1.at[n, i], b1s.at[n, i], b1r.at[n, i], y_peer(2 * i + 1 - n % 2))

    def a2_copy(q, dy):
        return remote(sa2.at[q, dy], ra2.at[q, dy], a2s.at[q, dy], a2r.at[q, dy], y_peer(dy))

    def b2_copy(q, dx):
        return remote(sb2.at[q, dx], rb2.at[q, dx], b2s.at[q, dx], b2r.at[q, dx], x_peer(dx))

    def z_copy(q, dz):
        zr, kk = q // 4, q % 4
        return remote(zsend.at[q, (zh + dz) % 4], rz.at[kk, zr * 4 + dz],
                      zs_sem.at[q, dz], zr_sem.at[q, dz], z_peer(dz, zr))

    def first_stage(n):
        chip_copy(n).wait_recv()
        for e in range(8):
            total = own[n, e, core] + rchip[n, e]
            rchip[n, e] = total
            sa1[n, e % 4, e // 4] = total[0:32].astype(BF)
            sb1[n, e // 4, e % 4] = total[32:64].astype(BF)
        for dx in range(1, 4):
            a1_copy(n, dx).start()
        b1_copy(n, 1).start()

        @pl.when(n % 2 == 0)
        def _():
            b1_copy(n, 0).start()

    def second_stage(q):
        for half in range(2):
            n = 2 * q + half
            for dx in range(1, 4):
                a1_copy(n, dx).wait_recv()
            for i in range(half, 2):
                b1_copy(n, i).wait_recv()
        for dy in range(4):
            n, i = 2 * q + 1 - dy % 2, dy // 2
            total = rchip[n, i * 4, 0:32]
            for dx in range(1, 4):
                total = total + ra1[n, dx, i].astype(F32)
            sa2[q, dy] = total
        for dx in range(4):
            total = rchip[2 * q + 1, dx, 32:64]
            for dy in range(1, 4):
                total = total + rb1[2 * q + 1 - dy % 2, dy // 2, dx].astype(F32)
            sb2[q, dx] = total
        for d in range(1, 4):
            a2_copy(q, d).start()
            b2_copy(q, d).start()

    def third_stage(q):
        for d in range(1, 4):
            a2_copy(q, d).wait_recv()
            b2_copy(q, d).wait_recv()
        low, high = sa2[q, 0], sb2[q, 0]
        for d in range(1, 4):
            low = low + ra2[q, d]
            high = high + rb2[q, d]
        zsend[q, 0] = low[0:16]
        zsend[q, 1] = low[16:32]
        zsend[q, 2] = high[0:16]
        zsend[q, 3] = high[16:32]
        zr, kk = q // 4, q % 4
        for dz in range(1, 4):
            z_copy(q, dz).start()

        @pl.when(zr == 1)
        def _():
            z_copy(q, 0).start()

        @pl.when(zr == 0)
        def _():
            rz[kk, 0] = zsend[q, zh]

    def step(n, carry):
        contract(n, xz_tiles, False)
        chip_copy(n).start()

        @pl.when(n >= 1)
        def _():
            first_stage(n - 1)

        @pl.when((n >= 4) & (n % 2 == 0))
        def _():
            second_stage((n - 4) // 2)

        @pl.when((n >= 7) & (n % 2 == 1))
        def _():
            third_stage((n - 7) // 2)

        return carry

    lax.fori_loop(0, PASSES, step, 0)

    second_stage(6)
    first_stage(15)
    third_stage(5)
    third_stage(6)
    second_stage(7)
    third_stage(7)

    for q in range(8):
        for dz in range(0 if q >= 4 else 1, 4):
            z_copy(q, dz).wait_recv()
    for kk in range(4):
        total = rz[kk, 0]
        for s in range(1, 8):
            total = total + rz[kk, s]
        out[kk] = total * WEIGHT

    def drain(n, carry):
        chip_copy(n).wait_send()
        for dx in range(1, 4):
            a1_copy(n, dx).wait_send()
        b1_copy(n, 1).wait_send()

        @pl.when(n % 2 == 0)
        def _():
            b1_copy(n, 0).wait_send()

        return carry

    lax.fori_loop(0, PASSES, drain, 0)
    for q in range(8):
        for d in range(1, 4):
            a2_copy(q, d).wait_send()
            b2_copy(q, d).wait_send()
        for dz in range(0 if q >= 4 else 1, 4):
            z_copy(q, dz).wait_send()


def per_device(modes, wall_grad):
    phi5 = jnp.transpose(modes, (3, 0, 1, 2, 4))
    wall = jnp.transpose(wall_grad, (3, 0, 1, 2, 4)).reshape(3, POINTS, M)
    vm = pl.BlockSpec(memory_space=pltpu.VMEM)
    dma = pltpu.SemaphoreType.DMA
    return pl.pallas_call(
        kernel,
        out_shape=jax.ShapeDtypeStruct((4, 16, M), F32),
        in_specs=[vm] * 3,
        out_specs=vm,
        scratch_shapes=[
            pltpu.VMEM((2, 3, 80, M), BF),
            pltpu.VMEM((3, 2, 3, 48, M), BF),
            pltpu.VMEM((3, 2, 3, 48, M), BF),
            pltpu.VMEM((3, 80, M), BF),
            pltpu.VMEM((3, 80, M), BF),
            pltpu.VMEM((72, 64, M), F32),
            pltpu.VMEM((2, 3, POINTS, M), BF),
            pltpu.VMEM((5, 3, M, 256), BF),
            pltpu.VMEM((14, 3, M, 256), F32),
            pltpu.VMEM((PASSES, 8, 2, 64, M), F32),
            pltpu.VMEM((PASSES, 8, 64, M), F32),
            pltpu.VMEM((PASSES, 4, 2, 32, M), BF),
            pltpu.VMEM((PASSES, 2, 4, 32, M), BF),
            pltpu.VMEM((PASSES, 4, 2, 32, M), BF),
            pltpu.VMEM((PASSES, 2, 4, 32, M), BF),
            pltpu.VMEM((8, 4, 32, M), F32),
            pltpu.VMEM((8, 4, 32, M), F32),
            pltpu.VMEM((8, 4, 32, M), F32),
            pltpu.VMEM((8, 4, 32, M), F32),
            pltpu.VMEM((8, 4, 16, M), F32),
            pltpu.VMEM((4, 8, 16, M), F32),
            dma((4,)), dma((4,)),
            dma((PASSES,)), dma((PASSES,)),
            dma((PASSES, 4)), dma((PASSES, 4)),
            dma((PASSES, 2)), dma((PASSES, 2)),
            dma((8, 4)), dma((8, 4)),
            dma((8, 4)), dma((8, 4)),
            dma((8, 4)), dma((8, 4)),
        ],
        compiler_params=pltpu.CompilerParams(
            collective_id=0, has_side_effects=True, vmem_limit_bytes=56 * 2**20),
        cost_estimate=pl.CostEstimate(
            flops=2 * 128 * 3456 * 16384, bytes_accessed=4 * 2**20, transcendentals=0),
    )(phi5.reshape(3, POINTS, M), phi5, wall)


def solution(mesh):
    placed = (P(None, "gx", "gz", None, None), P(None, "gx", "gz", None, None))
    body = jax.shard_map(
        per_device, mesh=mesh, in_specs=placed, out_specs=P("gx", "gz", None), check_vma=False)

    def run(modes, wall_grad):
        with jax.sharding.use_abstract_mesh(mesh.abstract_mesh):
            return body(modes, wall_grad)

    return run
```

time: 96.1 us -> 74.2 us (0.77)
  Pallas kernels: 88.8 us -> 68.4 us
  local copies, waits for them, and re-layouts: 5.78 us -> 4.61 us
    pallas_call x1, Pallas kernels: 88.8 us -> 68.4 us  [per_device(): pl.pallas_call(kernel, out_shape=jax.ShapeDtypeStruct((4, 16, M), F32), i...]
    another operation x1 -> x0, local copies, waits for them, and re-layouts: 1.13 us -> none  [per_device(): rows = jnp.stack([modes[:, :, 0:3], modes[:, :, 45:48]])]
    unnamed x6 -> x4, local copies, waits for them, and re-layouts: 2.87 us -> 3.61 us
where the time goes in v2:
time: 74.2 us; the launch traced here: 73.1 us
  Pallas kernels  68.4 us (92%)
  local copies, waits for them, and re-layouts  4.61 us (6%)
    pallas_call x1, Pallas kernels, per_device(): pl.pallas_call(kernel, out_shape=jax.ShapeDtypeStruct((4, 16, M), F32), i...  68.4 us
    unnamed x4, local copies, waits for them, and re-layouts  3.61 us

profile of v2, /device:TPU:24, one launch (start us, length us, event | category | flops | bytes accessed | tf_op | source)
XLA Modules:
  0.0 73.1 jit_solution(10946886190111773522)
XLA Ops:
  0.0 0.0 copy-start
  0.0 2.2 %copy.7 = bf16[2,12,48,3,128]{4,2,1,0,3:T(8,128)(2,1)} copy(bf16[2,12,48,3,128]{4,2,3,1,0:T(8,128)(2,1)} %param.2) | data formatting | bytes 1769472 | tf_op args[0]
  2.2 0.0 copy-done
  2.2 1.0 %copy.4 = bf16[3,2,12,48,128]{4,3,2,1,0:T(8,128)(2,1)} copy(bf16[3,2,12,48,128]{4,3,0,2,1:T(8,128)(2,1)S(1)} %bitcast.7) | data formatting | bytes 1769472 | tf_op jit(solution)/shard_map/transpose | solution.py:331
  3.2 68.4 %shard_map.28 = f32[4,16,128]{2,1,0:T(8,128)} custom-call(bf16[3,1152,128]{2,1,0:T(8,128)(2,1)} %bitcast.8, bf16[3,2,12,48,128]{4,3,2,1,0:T(8,128)(2,1)} %bitcast.9, bf16[3,1152,128]{2,1,0:T(8,128)(2,1)} %bitcast.10), custom_call_target="tpu_custom_call" | custom-call | flops 14495514624 | bytes 4194304 | tf_op jit(solution)/shard_map/pallas_call | solution.py:334
  71.7 1.4 %copy.9 = f32[4,16,128]{2,1,0:T(8,128)} copy(f32[4,16,128]{2,1,0:T(8,128)} %shard_map.28) | data formatting | bytes 65536
Async XLA Ops:
  0.0 2.2 %copy-start = (bf16[2,12,48,3,128]{4,2,3,1,0:T(8,128)(2,1)S(1)}, bf16[2,12,48,3,128]{4,2,3,1,0:T(8,128)(2,1)}, u32[]{:S(2)}) copy-start(bf16[2,12,48,3,128]{4,2,3,1,0:T(8,128)(2,1)} %param.3) | copy-start | bytes 2654212

commit v3 on v2

--- a/solution.py
+++ b/solution.py
@@ -18,7 +18,7 @@
 EARLY = 5
 
 
-def kernel(phi, phi5, wall, out,
+def kernel(phi5, wall5, out,
            edges, xlo, xhi, zlo, zhi, zpad, gnat, phil, gt, own, rchip,
            sa1, sb1, ra1, rb1, sa2, sb2, ra2, rb2, zsend, rz,
            hs_sem, hr_sem, cs_sem, cr_sem, a1s, a1r, b1s, b1r, a2s, a2r, b2s, b2r, zs_sem, zr_sem):
@@ -52,6 +52,18 @@
     for peer in peers:
         pl.semaphore_signal(barrier, inc=1, device_id=peer, device_id_type=MESH)
 
+    def cells(ref, c, lo, size):
+        pieces, end = [], lo + size
+        while lo < end:
+            slab, start = lo // 48, lo % 48
+            count = min(48 - start, end - lo)
+            pieces.append(ref[slab // 12, slab % 12, c, start:start + count, :])
+            lo += count
+        return pieces
+
+    def turned(ref, c, lo):
+        return jnp.concatenate([p.astype(F32) for p in cells(ref, c, lo, M)], axis=0).T
+
     def remote(src, dst, ss, rs, dev):
         return pltpu.make_async_remote_copy(
             src_ref=src, dst_ref=dst, send_sem=ss, recv_sem=rs, device_id=dev, device_id_type=MESH)
@@ -60,19 +72,19 @@
     for c in range(3):
         for b in range(4):
             for h in range(2):
-                rows = slice(b * 256 + h * 128, b * 256 + h * 128 + 128)
-                phil[b, c, :, h * 128:h * 128 + 128] = phi[c, rows, :].astype(F32).T.astype(BF)
-                gt[b, c, :, h * 128:h * 128 + 128] = wall[c, rows, :].astype(F32).T
-        tail = phi[c, 1024:1152, :].astype(F32).T.astype(BF)
+                spot = slice(h * 128, h * 128 + 128)
+                phil[b, c, :, spot] = turned(phi5, c, b * 256 + h * 128).astype(BF)
+                gt[b, c, :, spot] = turned(wall5, c, b * 256 + h * 128)
+        tail = turned(phi5, c, 1024).astype(BF)
         phil[4, c, :, 0:128] = tail
         phil[4, c, :, 128:256] = tail
-        gt[4, c, :, 0:128] = wall[c, 1024:1152, :].astype(F32).T
+        gt[4, c, :, 0:128] = turned(wall5, c, 1024)
         gt[4, c, :, 128:256] = zero
 
     def fill(s, carry):
         c, p = s // 2, s % 2
         for x in range(12):
-            zpad[s * 12 + x, 8:56, :] = phi5[c, p, x].astype(F32)
+            zpad[s * 12 + x, 8:56, :] = phi5[p, x, c].astype(F32)
         return carry
 
     lax.fori_loop(0, 6, fill, 0)
@@ -96,11 +108,11 @@
 
         def scoped(*accs):
             for t, left, parts in tiles:
-                block = [phi[a, lo:lo + size, :] for a, lo, size in parts]
+                block = [p for a, lo, size in parts for p in cells(phi5, a, lo, size)]
                 size = sum(p[2] for p in parts)
                 if size < 256:
                     block.append(jnp.zeros((256 - size, M), BF))
-                block = jnp.concatenate(block, axis=0) if len(block) > 1 else block[0]
+                block = jnp.concatenate(block, axis=0)
                 block = jnp.concatenate([block, jnp.zeros((256, M), BF)], axis=1)
                 for m in (0, 1):
                     pltpu.matmul_push_rhs(block, 0, m)
@@ -138,8 +150,8 @@
     lax.fori_loop(0, EARLY, wall_pass, 0)
     pl.semaphore_wait(barrier, len(peers))
     halos = [
-        remote(phi5.at[:, :, 9:12], xlo, hs_sem.at[0], hr_sem.at[0], x_next),
-        remote(phi5.at[:, :, 0:3], xhi, hs_sem.at[1], hr_sem.at[1], x_prev),
+        remote(phi5.at[:, 9:12], xlo, hs_sem.at[0], hr_sem.at[0], x_next),
+        remote(phi5.at[:, 0:3], xhi, hs_sem.at[1], hr_sem.at[1], x_prev),
         remote(edges.at[1], zlo, hs_sem.at[2], hr_sem.at[2], z_next),
         remote(edges.at[0], zhi, hs_sem.at[3], hr_sem.at[3], z_prev),
     ]
@@ -160,10 +172,10 @@
 
         def at(x):
             if x < 0:
-                return xlo[c, p, x + 3].astype(F32)
+                return xlo[p, x + 3, c].astype(F32)
             if x >= 12:
-                return xhi[c, p, x - 12].astype(F32)
-            return phi5[c, p, x].astype(F32)
+                return xhi[p, x - 12, c].astype(F32)
+            return phi5[p, x, c].astype(F32)
 
         for x in range(12):
             total = jnp.zeros((48, M), F32)
@@ -208,13 +220,15 @@
         return remote(zsend.at[q, (zh + dz) % 4], rz.at[kk, zr * 4 + dz],
                       zs_sem.at[q, dz], zr_sem.at[q, dz], z_peer(dz, zr))
 
-    def first_stage(n):
+    def chip_sum(n):
         chip_copy(n).wait_recv()
         for e in range(8):
             total = own[n, e, core] + rchip[n, e]
             rchip[n, e] = total
             sa1[n, e % 4, e // 4] = total[0:32].astype(BF)
             sb1[n, e // 4, e % 4] = total[32:64].astype(BF)
+
+    def first_stage(n):
         for dx in range(1, 4):
             a1_copy(n, dx).start()
         b1_copy(n, 1).start()
@@ -270,30 +284,39 @@
             rz[kk, 0] = zsend[q, zh]
 
     def step(n, carry):
+        chip_sum(n - 2)
         contract(n, xz_tiles, False)
         chip_copy(n).start()
-
-        @pl.when(n >= 1)
-        def _():
-            first_stage(n - 1)
-
-        @pl.when((n >= 4) & (n % 2 == 0))
-        def _():
-            second_stage((n - 4) // 2)
-
-        @pl.when((n >= 7) & (n % 2 == 1))
-        def _():
-            third_stage((n - 7) // 2)
-
-        return carry
-
-    lax.fori_loop(0, PASSES, step, 0)
-
+        first_stage(n - 2)
+
+        @pl.when((n >= 6) & (n % 2 == 0))
+        def _():
+            second_stage((n - 6) // 2)
+
+        @pl.when((n >= 9) & (n % 2 == 1))
+        def _():
+            third_stage((n - 9) // 2)
+
+        return carry
+
+    def opening(n, carry):
+        contract(n, xz_tiles, False)
+        chip_copy(n).start()
+        return carry
+
+    lax.fori_loop(0, 2, opening, 0)
+    lax.fori_loop(2, PASSES, step, 0)
+    chip_sum(14)
+    first_stage(14)
+
+    second_stage(5)
+    third_stage(4)
+    chip_sum(15)
+    first_stage(15)
     second_stage(6)
-    first_stage(15)
     third_stage(5)
+    second_stage(7)
     third_stage(6)
-    second_stage(7)
     third_stage(7)
 
     for q in range(8):
@@ -327,19 +350,19 @@
 
 
 def per_device(modes, wall_grad):
-    phi5 = jnp.transpose(modes, (3, 0, 1, 2, 4))
-    wall = jnp.transpose(wall_grad, (3, 0, 1, 2, 4)).reshape(3, POINTS, M)
+    phi5 = jnp.transpose(modes, (0, 1, 3, 2, 4))
+    wall5 = jnp.transpose(wall_grad, (0, 1, 3, 2, 4))
     vm = pl.BlockSpec(memory_space=pltpu.VMEM)
     dma = pltpu.SemaphoreType.DMA
     return pl.pallas_call(
         kernel,
         out_shape=jax.ShapeDtypeStruct((4, 16, M), F32),
-        in_specs=[vm] * 3,
+        in_specs=[vm] * 2,
         out_specs=vm,
         scratch_shapes=[
             pltpu.VMEM((2, 3, 80, M), BF),
-            pltpu.VMEM((3, 2, 3, 48, M), BF),
-            pltpu.VMEM((3, 2, 3, 48, M), BF),
+            pltpu.VMEM((2, 3, 3, 48, M), BF),
+            pltpu.VMEM((2, 3, 3, 48, M), BF),
             pltpu.VMEM((3, 80, M), BF),
             pltpu.VMEM((3, 80, M), BF),
             pltpu.VMEM((72, 64, M), F32),
@@ -370,7 +393,7 @@
             collective_id=0, has_side_effects=True, vmem_limit_bytes=56 * 2**20),
         cost_estimate=pl.CostEstimate(
             flops=2 * 128 * 3456 * 16384, bytes_accessed=4 * 2**20, transcendentals=0),
-    )(phi5.reshape(3, POINTS, M), phi5, wall)
+    )(phi5, wall5)
 
 
 def solution(mesh):

time: 74.2 us -> 68.2 us (0.919)
  local copies, waits for them, and re-layouts: 4.61 us -> 1.38 us
  Pallas kernels: 68.4 us -> 66.4 us
    unnamed x4 -> x1, local copies, waits for them, and re-layouts: 3.61 us -> 1.38 us
    pallas_call x1, Pallas kernels: 68.4 us -> 66.4 us  [per_device(): pl.pallas_call(kernel, out_shape=jax.ShapeDtypeStruct((4, 16, M), F32), i...]
    transpose x1 -> x0, local copies, waits for them, and re-layouts: 1 us -> none  [per_device(): wall = jnp.transpose(wall_grad, (3, 0, 1, 2, 4)).reshape(3, POINTS, M)]
where the time goes in v3:
time: 68.2 us; the launch traced here: 67.8 us
  Pallas kernels  66.4 us (97%)
  local copies, waits for them, and re-layouts  1.38 us (2%)
    pallas_call x1, Pallas kernels, per_device(): pl.pallas_call(kernel, out_shape=jax.ShapeDtypeStruct((4, 16, M), F32), i...  66.4 us
    unnamed x1, local copies, waits for them, and re-layouts  1.38 us

profile of v3, /device:TPU:24, one launch (start us, length us, event | category | flops | bytes accessed | tf_op | source)
XLA Modules:
  0.0 67.8 jit_solution(1695260053250786988)
XLA Ops:
  0.0 66.4 %shard_map.28 = f32[4,16,128]{2,1,0:T(8,128)} custom-call(bf16[2,12,3,48,128]{4,3,2,1,0:T(8,128)(2,1)} %bitcast.2, bf16[2,12,3,48,128]{4,3,2,1,0:T(8,128)(2,1)} %bitcast.3), custom_call_target="tpu_custom_call" | custom-call | flops 14495514624 | bytes 4194304 | tf_op jit(solution)/shard_map/pallas_call | solution.py:357
  66.4 1.4 %copy.4 = f32[4,16,128]{2,1,0:T(8,128)} copy(f32[4,16,128]{2,1,0:T(8,128)} %shard_map.28) | data formatting | bytes 65536

commit v4 on v3

--- a/solution.py
+++ b/solution.py
@@ -15,7 +15,7 @@
 WEIGHT = 1.0 / math.sqrt(2 * 384 * 384)
 POINTS = 1152
 PASSES = 16
-EARLY = 5
+EARLY = 4
 
 
 def kernel(phi5, wall5, out,
@@ -96,7 +96,7 @@
 
     def modes_of(n):
         q, half = n // 2, n % 2
-        zr, kk = q // 4, q % 4
+        zr, kk = 1 - q // 4, q % 4
         ks = []
         for e in range(8):
             dx, dy = e % 4, 2 * (e // 4) + 1 - half
@@ -144,10 +144,11 @@
     xz_tiles.append((13, 4, [(0, 1024, 128), (2, 1024, 128)]))
 
     def wall_pass(n, carry):
-        contract(n, y_tiles, True)
-        return carry
-
-    lax.fori_loop(0, EARLY, wall_pass, 0)
+        contract(2 * n, y_tiles, True)
+        contract(2 * n + 1, y_tiles, True)
+        return carry
+
+    lax.fori_loop(0, EARLY // 2, wall_pass, 0)
     pl.semaphore_wait(barrier, len(peers))
     halos = [
         remote(phi5.at[:, 9:12], xlo, hs_sem.at[0], hr_sem.at[0], x_next),
@@ -157,7 +158,7 @@
     ]
     for h in halos:
         h.start()
-    lax.fori_loop(EARLY, PASSES, wall_pass, 0)
+    lax.fori_loop(EARLY // 2, PASSES // 2, wall_pass, 0)
     for h in halos:
         h.wait()
 
@@ -216,7 +217,7 @@
         return remote(sb2.at[q, dx], rb2.at[q, dx], b2s.at[q, dx], b2r.at[q, dx], x_peer(dx))
 
     def z_copy(q, dz):
-        zr, kk = q // 4, q % 4
+        zr, kk = 1 - q // 4, q % 4
         return remote(zsend.at[q, (zh + dz) % 4], rz.at[kk, zr * 4 + dz],
                       zs_sem.at[q, dz], zr_sem.at[q, dz], z_peer(dz, zr))
 
@@ -271,7 +272,7 @@
         zsend[q, 1] = low[16:32]
         zsend[q, 2] = high[0:16]
         zsend[q, 3] = high[16:32]
-        zr, kk = q // 4, q % 4
+        zr, kk = 1 - q // 4, q % 4
         for dz in range(1, 4):
             z_copy(q, dz).start()
 
@@ -283,19 +284,25 @@
         def _():
             rz[kk, 0] = zsend[q, zh]
 
-    def step(n, carry):
+    def steps(m, carry):
+        n = 2 * m
         chip_sum(n - 2)
         contract(n, xz_tiles, False)
         chip_copy(n).start()
         first_stage(n - 2)
 
-        @pl.when((n >= 6) & (n % 2 == 0))
-        def _():
-            second_stage((n - 6) // 2)
-
-        @pl.when((n >= 9) & (n % 2 == 1))
-        def _():
-            third_stage((n - 9) // 2)
+        @pl.when(n >= 6)
+        def _():
+            second_stage(m - 3)
+
+        chip_sum(n - 1)
+        contract(n + 1, xz_tiles, False)
+        chip_copy(n + 1).start()
+        first_stage(n - 1)
+
+        @pl.when(n >= 8)
+        def _():
+            third_stage(m - 4)
 
         return carry
 
@@ -305,7 +312,7 @@
         return carry
 
     lax.fori_loop(0, 2, opening, 0)
-    lax.fori_loop(2, PASSES, step, 0)
+    lax.fori_loop(1, PASSES // 2, steps, 0)
     chip_sum(14)
     first_stage(14)
 
@@ -320,7 +327,7 @@
     third_stage(7)
 
     for q in range(8):
-        for dz in range(0 if q >= 4 else 1, 4):
+        for dz in range(0 if q < 4 else 1, 4):
             z_copy(q, dz).wait_recv()
     for kk in range(4):
         total = rz[kk, 0]
@@ -345,7 +352,7 @@
         for d in range(1, 4):
             a2_copy(q, d).wait_send()
             b2_copy(q, d).wait_send()
-        for dz in range(0 if q >= 4 else 1, 4):
+        for dz in range(0 if q < 4 else 1, 4):
             z_copy(q, dz).wait_send()
 
 

time: 68.2 us -> 67.2 us (0.985)
  Pallas kernels: 66.4 us -> 65.6 us
    pallas_call x1, Pallas kernels: 66.4 us -> 65.6 us  [per_device(): pl.pallas_call(kernel, out_shape=jax.ShapeDtypeStruct((4, 16, M), F32), i...]
where the time goes in v4:
time: 67.2 us; the launch traced here: 67 us
  Pallas kernels  65.6 us (98%)
  local copies, waits for them, and re-layouts  1.38 us (2%)
    pallas_call x1, Pallas kernels, per_device(): pl.pallas_call(kernel, out_shape=jax.ShapeDtypeStruct((4, 16, M), F32), i...  65.6 us
    unnamed x1, local copies, waits for them, and re-layouts  1.38 us

profile of v4, /device:TPU:24, one launch (start us, length us, event | category | flops | bytes accessed | tf_op | source)
XLA Modules:
  0.0 67.0 jit_solution(18168909051823347766)
XLA Ops:
  0.0 65.6 %shard_map.28 = f32[4,16,128]{2,1,0:T(8,128)} custom-call(bf16[2,12,3,48,128]{4,3,2,1,0:T(8,128)(2,1)} %bitcast.2, bf16[2,12,3,48,128]{4,3,2,1,0:T(8,128)(2,1)} %bitcast.3), custom_call_target="tpu_custom_call" | custom-call | flops 14495514624 | bytes 4194304 | tf_op jit(solution)/shard_map/pallas_call | solution.py:364
  65.7 1.4 %copy.4 = f32[4,16,128]{2,1,0:T(8,128)} copy(f32[4,16,128]{2,1,0:T(8,128)} %shard_map.28) | data formatting | bytes 65536

commit v5 on v4

--- a/solution.py
+++ b/solution.py
@@ -15,7 +15,7 @@
 WEIGHT = 1.0 / math.sqrt(2 * 384 * 384)
 POINTS = 1152
 PASSES = 16
-EARLY = 4
+EARLY = 6
 
 
 def kernel(phi5, wall5, out,

time: 67.2 us -> 69 us (1.027)
  Pallas kernels: 65.6 us -> 67.5 us
    pallas_call x1, Pallas kernels: 65.6 us -> 67.5 us  [per_device(): pl.pallas_call(kernel, out_shape=jax.ShapeDtypeStruct((4, 16, M), F32), i...]
where the time goes in v5:
time: 69 us; the launch traced here: 68.8 us
  Pallas kernels  67.5 us (98%)
  local copies, waits for them, and re-layouts  1.38 us (2%)
    pallas_call x1, Pallas kernels, per_device(): pl.pallas_call(kernel, out_shape=jax.ShapeDtypeStruct((4, 16, M), F32), i...  67.5 us

profile of v5, /device:TPU:24, one launch (start us, length us, event | category | flops | bytes accessed | tf_op | source)
XLA Modules:
  0.0 68.8 jit_solution(9549279227153210917)
XLA Ops:
  0.0 67.5 %shard_map.28 = f32[4,16,128]{2,1,0:T(8,128)} custom-call(bf16[2,12,3,48,128]{4,3,2,1,0:T(8,128)(2,1)} %bitcast.2, bf16[2,12,3,48,128]{4,3,2,1,0:T(8,128)(2,1)} %bitcast.3), custom_call_target="tpu_custom_call" | custom-call | flops 14495514624 | bytes 4194304 | tf_op jit(solution)/shard_map/pallas_call | solution.py:364
  67.5 1.4 %copy.4 = f32[4,16,128]{2,1,0:T(8,128)} copy(f32[4,16,128]{2,1,0:T(8,128)} %shard_map.28) | data formatting | bytes 65536
